TPU v7x, 32 devices: a whole 2x2x4 slice. The times are simulated.
32 devices in a mesh: seq: 8 (over z, x), tp: 4 (over y, core).
Axes of the slice: x: 2, y: 2, z: 4, core: 2. Of those that a mesh axis runs over, the one named last changes fastest.
Arguments:
- queries: bfloat16 [2048, 8192], P('seq', 'tp'), may hold values from -6 to 6
- keys: bfloat16 [2048, 8192], P('seq', 'tp'), may hold values from -6 to 6
- values: bfloat16 [2048, 8192], P('seq', 'tp'), may hold values from -6 to 6
- norm_gain: float32 [128], replicated, may hold values from 0.1 to 1.9
- out_weight: bfloat16 [8192, 8192], P(None, 'tp'), may hold values from -0.0625 to 0.0625
Outputs:
- layer_out: bfloat16 [2048, 8192], P('seq', 'tp')
All inputs are finite; a program needn't handle non-finite values.
Results may differ from a plain program's by a relative error of at most 0.0058.
Values may be sent and summed in bfloat16 or wider, within the bound.
A program may use at most 128 MiB of HBM per device.

v0:
```python
import jax
import jax.numpy as jnp
from jax import lax
from jax.sharding import PartitionSpec as P

DH = 128


epsilon = 1e-06


def from_behind(x, axis, by):
    length = lax.axis_size(axis)
    pairs = [(i, i + by) for i in range(length) if 0 <= i + by < length]
    return lax.ppermute(x, axis, pairs)


def on_device(queries, keys, values, norm_gain, out_weight):
    tok_rows = queries.shape[0]
    head_count = queries.shape[1] // DH
    query_head_rows = queries.reshape(tok_rows, head_count, DH)
    key_head_rows = keys.reshape(tok_rows, head_count, DH)
    value_head_rows = values.reshape(tok_rows, head_count, DH)
    segment_state = jnp.einsum(
        "ncf,ncq->cfq", key_head_rows, value_head_rows, preferred_element_type=jnp.float32
    )
    inclusive = segment_state
    seq_width = lax.axis_size("seq")
    doubling_rounds = (seq_width - 1).bit_length()
    for section_index in range(doubling_rounds):
        inclusive = inclusive + from_behind(inclusive, "seq", 1 << section_index)
    prefix = inclusive - segment_state
    prefix_batch = prefix.astype(jnp.bfloat16)
    carried_state = jnp.einsum(
        "jza,zaq->jzq", query_head_rows, prefix_batch, preferred_element_type=jnp.float32
    )
    scores = jnp.einsum(
        "thk,shk->hts", query_head_rows, key_head_rows, preferred_element_type=jnp.float32
    )
    row_ids = lax.broadcasted_iota(jnp.int32, (tok_rows, tok_rows), 0)
    col_ids = lax.broadcasted_iota(jnp.int32, (tok_rows, tok_rows), 1)
    causal = col_ids <= row_ids
    scores_b = jnp.where(causal[None], scores, jnp.float32(0.0)).astype(jnp.bfloat16)
    within = jnp.einsum(
        "hts,shv->thv", scores_b, value_head_rows, preferred_element_type=jnp.float32
    )
    attended = carried_state + within
    inverse = lax.rsqrt(jnp.mean(attended * attended, axis=-1, keepdims=True) + epsilon)
    normed = (
        (attended * inverse * norm_gain).astype(jnp.bfloat16).reshape(tok_rows, head_count * DH)
    )
    collected_states = lax.all_gather(normed, "tp", axis=1, tiled=True)
    summed = jnp.dot(collected_states, out_weight, preferred_element_type=jnp.float32)
    return summed.astype(jnp.bfloat16)


def solution(mesh):
    return jax.shard_map(
        on_device,
        mesh=mesh,
        in_specs=(P("seq", "tp"), P("seq", "tp"), P("seq", "tp"), P(), P(None, "tp")),
        out_specs=P("seq", "tp"),
        check_vma=False,
    )
```

profile of v0, /device:TPU:25, one launch (start us, length us, event | category | flops | bytes accessed | tf_op | source)
XLA Modules:
  0.0 177.9 jit_solution(11382472696715363967)
XLA Ops:
  6.5 0.0 copy-start
  6.5 0.0 copy-start.1
  6.5 0.0 all-gather.2.cloned.1.call-start
  6.5 1.6 copy.13
  8.2 0.0 copy-done.1
  8.2 1.3 copy.12
  9.5 1.7 fusion.8
  11.1 3.1 %collective-permute-start = (f32[16,128,128]{2,1,0:T(8,128)S(1)}, f32[16,128,128]{2,1,0:T(8,128)S(1)}, u32[]{:S(2)}, u32[]{:S(2)}) collective-permute-start(f32[16,128,128]{2,1,0:T(8,128)S(1)} %fusion.8), channel_id=1, source_target_pairs={{0,4},{4,8},{8,12},{12,16},{16,20},{20,24},{24,28},{1,5},{5,9},{9,... | collective-permute-start | bytes 3145736 | tf_op jit(solution)/shard_map/ppermute | solution.py:15
  14.3 23.7 %collective-permute-done = f32[16,128,128]{2,1,0:T(8,128)S(1)} collective-permute-done((f32[16,128,128]{2,1,0:T(8,128)S(1)}, f32[16,128,128]{2,1,0:T(8,128)S(1)}, u32[]{:S(2)}, u32[]{:S(2)}) %collective-permute-start) | collective-permute-done | bytes 1048608 | tf_op jit(solution)/shard_map/ppermute | solution.py:15
  38.0 0.1 add.23
  38.1 1.3 collective-permute-start.1
  39.4 23.7 %collective-permute-done.1 = f32[16,128,128]{2,1,0:T(8,128)S(1)} collective-permute-done((f32[16,128,128]{2,1,0:T(8,128)S(1)}, f32[16,128,128]{2,1,0:T(8,128)S(1)}, u32[]{:S(2)}, u32[]{:S(2)}) %collective-permute-start.1) | collective-permute-done | bytes 1048608 | tf_op jit(solution)/shard_map/ppermute | solution.py:15
  63.1 1.1 add.24
  64.2 1.3 collective-permute-start.2
  65.5 0.0 copy-done
  65.5 3.9 %fusion = f32[16,256,128]{1,2,0:T(8,128)} fusion(bf16[256,16,128]{0,2,1:T(8,128)(2,1)S(1)} %bitcast.30, bf16[256,16,128]{0,2,1:T(8,128)(2,1)} %bitcast.32, pred[256,256]{1,0:T(8,128)(4,1)S(1)} %iota_compare_fusion, bf16[256,2048]{1,0:T(8,128)(2,1)S(1)} %copy-done), kind=kOutput, calls=%fused_computation.5 | convolution fusion | flops 538968064 | bytes 5308416 | tf_op jit(solution)/shard_map/hts,shv->thv/dot_general | solution.py:44
  69.4 0.0 copy-start.2
  69.4 45.3 %collective-permute-done.2 = f32[16,128,128]{2,1,0:T(8,128)} collective-permute-done((f32[16,128,128]{2,1,0:T(8,128)}, f32[16,128,128]{2,1,0:T(8,128)}, u32[]{:S(2)}, u32[]{:S(2)}) %collective-permute-start.2) | collective-permute-done | bytes 1048608 | tf_op jit(solution)/shard_map/ppermute | solution.py:15
  114.7 2.8 %multiply_reduce_fusion = (f32[256,16]{0,1:T(8,128)S(1)}, f32[256,16,128]{0,2,1:T(8,128)S(1)}) fusion(f32[16,256,128]{1,2,0:T(8,128)} %fusion, f32[16,128,128]{2,1,0:T(8,128)S(1)} %fusion.8, f32[16,128,128]{2,1,0:T(8,128)} %add.24, f32[16,128,128]{2,1,0:T(8,128)} %collective-permute-done.2, bf16[256,2048]{1,0:T(8,128)(2,1)S(1)} %copy-done), kind=kOutput, calls=%fused_computation.4 | convolution fusion | flops 136572928 | bytes 8404992 | tf_op jit(solution)/shard_map/jza,zaq->jzq/dot_general | solution.py:34
  117.6 0.0 copy-done.2
  117.6 1.5 multiply_convert_fusion
  119.1 0.0 all-gather.2.cloned.1.call-update
  119.1 34.9 %all-gather.2.cloned.1.call-done = bf16[256,8192]{0,1:T(8,128)(2,1)} async-done(((bf16[256,2048]{0,1:T(8,128)(2,1)}), bf16[256,8192]{0,1:T(8,128)(2,1)}) %all-gather.2.cloned.1.call-update) | async-done | bytes 4194320 | tf_op jit(solution)/shard_map/all_gather | solution.py:52
  154.0 17.0 %convolution_convert_fusion = bf16[256,2048]{1,0:T(8,128)(2,1)} fusion(bf16[256,8192]{0,1:T(8,128)(2,1)} %all-gather.2.cloned.1.call-done, bf16[8192,2048]{1,0:T(8,128)(2,1)} %param.9), kind=kOutput, calls=%fused_computation.1 | convolution fusion | flops 8590458880 | bytes 38797312 | tf_op jit(solution)/shard_map/dot_general | solution.py:53
  (2 shorter events, 0.0 us)
Async XLA Ops:
  6.5 59.0 %copy-start = (bf16[256,2048]{1,0:T(8,128)(2,1)S(1)}, bf16[256,2048]{1,0:T(8,128)(2,1)}, u32[]{:S(2)}) copy-start(bf16[256,2048]{1,0:T(8,128)(2,1)} %param.5) | copy-start | bytes 3145732
  6.5 1.6 copy-start.1
  6.5 147.5 %all-gather.2.cloned.1.call-start = ((), (), s32[]{:S(2)}) async-start(), calls=%async_computation | async-start | bytes 5242880 | tf_op jit(solution)/shard_map/all_gather | solution.py:52
  11.1 26.8 %collective-permute-start = (f32[16,128,128]{2,1,0:T(8,128)S(1)}, f32[16,128,128]{2,1,0:T(8,128)S(1)}, u32[]{:S(2)}, u32[]{:S(2)}) collective-permute-start(f32[16,128,128]{2,1,0:T(8,128)S(1)} %fusion.8), channel_id=1, source_target_pairs={{0,4},{4,8},{8,12},{12,16},{16,20},{20,24},{24,28},{1,5},{5,9},{9,... | collective-permute-start | bytes 3145736 | tf_op jit(solution)/shard_map/ppermute | solution.py:15
  38.1 25.0 %collective-permute-start.1 = (f32[16,128,128]{2,1,0:T(8,128)S(1)}, f32[16,128,128]{2,1,0:T(8,128)S(1)}, u32[]{:S(2)}, u32[]{:S(2)}) collective-permute-start(f32[16,128,128]{2,1,0:T(8,128)S(1)} %add.23), channel_id=1, source_target_pairs={{0,8},{4,12},{8,16},{12,20},{16,24},{20,28},{1,9},{5,13},{9,17},{1... | collective-permute-start | bytes 3145736 | tf_op jit(solution)/shard_map/ppermute | solution.py:15
  64.2 50.6 %collective-permute-start.2 = (f32[16,128,128]{2,1,0:T(8,128)}, f32[16,128,128]{2,1,0:T(8,128)}, u32[]{:S(2)}, u32[]{:S(2)}) collective-permute-start(f32[16,128,128]{2,1,0:T(8,128)} %add.24), channel_id=1, source_target_pairs={{0,16},{4,20},{8,24},{12,28},{1,17},{5,21},{9,25},{13,29},{2,18},{... | collective-permute-start | bytes 3145736 | tf_op jit(solution)/shard_map/ppermute | solution.py:15
  69.4 48.2 %copy-start.2 = (f32[128]{0:T(128)S(1)}, f32[128]{0:T(128)}, u32[]{:S(2)}) copy-start(f32[128]{0:T(128)} %param.8) | copy-start | bytes 1540
Sparse Core Ops, SparseCore 0:
  119.2 34.7 all-gather.1
where the time goes:
time: 179 us; the launch traced here: 178 us
  waiting for transfers between devices  128 us (72%)
  matrix products  25.4 us (14%)
  between operations  13.5 us (8%)
  starting transfers between devices  5.7 us (3%)
  local copies, waits for them, and re-layouts  2.94 us (2%)
  other arithmetic  2.77 us (2%)
    ppermute x3, waiting for transfers between devices, from_behind(): return lax.ppermute(x, axis, pairs)  92.7 us
    all_gather x1, waiting for transfers between devices, on_device(): collected_states = lax.all_gather(normed, 'tp', axis=1, tiled=True)  34.9 us
    dot_general x1, matrix products, on_device(): jnp.dot(collected_states, out_weight, preferred_element_type=jnp.float32)  17 us
    ppermute x3, starting transfers between devices, from_behind(): return lax.ppermute(x, axis, pairs)  5.69 us
    dot_general x1, matrix products, on_device(): jnp.einsum('hts,shv->thv', scores_b, value_head_rows, preferred_element_t...  3.9 us
  transfers between devices with their start and end apart: 4, of which 4 were waited for; matrix products, arithmetic and copies ran while one was open for 2% of the time, Pallas kernels for 0%

commit v1 on v0

v1 whole, which is shorter than its diff:
```python
import functools

import jax
import jax.numpy as jnp
from jax import lax
from jax.experimental import pallas as pl
from jax.experimental.pallas import tpu as pltpu
from jax.sharding import PartitionSpec as P

DH = 128
PACK = 2
INNER = 2
EPSILON = 1e-06
MESH = pl.DeviceIdType.MESH
F32 = jnp.float32
BF16 = jnp.bfloat16


def kernel(
    n_seq, n_tp,
    q_hbm, k_hbm, v_hbm, gain_ref, w_hbm, o_ref,
    q_buf, k_buf, v_buf, w_buf, state, x_out, x_in, z_out, z_in, within, normed, acc,
    qkv_sem, w_sem, x_send, x_recv, z_send, z_recv, sib_send, y_send, fwd_send, n_recv,
):
    n_chunks, rows, width = q_buf.shape
    n_out = n_seq // INNER
    n_y = n_tp // 2
    s = lax.axis_index("seq")
    t = lax.axis_index("tp")
    inner, outer = lax.rem(s, INNER), lax.div(s, INNER)
    core, y = lax.rem(t, 2), lax.div(t, 2)
    partner = s + 1 - 2 * inner
    sibling = t + 1 - 2 * core
    has_before = outer > 0
    has_after = outer < n_out - 1
    ahead = [lax.rem(y + d, n_y) * 2 + core for d in range(1, n_y)]
    behind = [lax.rem(y + n_y - d, n_y) * 2 + core for d in range(1, n_y)]
    behind_sib = [lax.rem(y + n_y - d, n_y) * 2 + 1 - core for d in range(1, n_y)]

    def load(which, g):
        src = (k_hbm, v_hbm, q_hbm)[which]
        dst = (k_buf, v_buf, q_buf)[which]
        cols = pl.ds(pl.multiple_of(g * width, width), width)
        return pltpu.make_async_copy(src.at[:, cols], dst.at[g], qkv_sem.at[which, g])

    def load_w(origin, g):
        at = origin * n_chunks + g
        span = pl.ds(pl.multiple_of(at * width, width), width)
        return pltpu.make_async_copy(w_hbm.at[span, :], w_buf.at[at], w_sem.at[at])

    def remote(src, dst, send, recv, seq_to, tp_to):
        return pltpu.make_async_remote_copy(
            src_ref=src, dst_ref=dst, send_sem=send, recv_sem=recv,
            device_id=(seq_to, tp_to), device_id_type=MESH,
        )

    def copy_x(g):
        return remote(x_out.at[g], x_in.at[g], x_send.at[g], x_recv.at[g], partner, t)

    def copy_z(g):
        after = jnp.minimum(s + INNER, n_seq - 1)
        return remote(z_out.at[g], z_in.at[g], z_send.at[g], z_recv.at[g], after, t)

    def copy_sib(g):
        return remote(normed.at[t, g], normed.at[t, g], sib_send.at[g], n_recv.at[t, g], s, sibling)

    def copy_y(d, g):
        return remote(normed.at[t, g], normed.at[t, g], y_send.at[d, g], n_recv.at[t, g], s, ahead[d])

    def copy_fwd(d, g):
        o = behind[d]
        return remote(normed.at[o, g], normed.at[o, g], fwd_send.at[d, g], n_recv.at[o, g], s, sibling)

    def arrived(o, g):
        return remote(normed.at[o, g], normed.at[o, g], sib_send.at[g], n_recv.at[o, g], s, sibling)

    def start_kv(g, _):
        load(0, g).start()
        load(1, g).start()
        return 0

    lax.fori_loop(0, n_chunks, start_kv, 0)

    barrier = pltpu.get_barrier_semaphore()
    for who in [(partner, t), (s, sibling)] + [(s, b) for b in behind]:
        pl.semaphore_signal(barrier, inc=1, device_id=who, device_id_type=MESH)

    @pl.when(has_before)
    def _():
        pl.semaphore_signal(barrier, inc=1, device_id=(s - INNER, t), device_id_type=MESH)

    def start_q(g, _):
        load(2, g).start()
        return 0

    lax.fori_loop(0, n_chunks, start_q, 0)

    pl.semaphore_wait(barrier, 1 + n_y + jnp.where(has_after, 1, 0))

    def make_state(g, _):
        load(0, g).wait()
        load(1, g).wait()
        for h in range(PACK):
            cols = pl.ds(h * DH, DH)
            own = lax.dot_general(
                k_buf[g, :, cols], v_buf[g, :, cols], (((0,), (0,)), ((), ())),
                preferred_element_type=F32,
            )
            state[g, h] = own
            x_out[g, h] = own.astype(x_out.dtype)
        copy_x(g).start()
        return 0

    lax.fori_loop(0, n_chunks, make_state, 0)

    def wait_q(g, _):
        load(2, g).wait()
        return 0

    def start_w(origins):
        def body(g, _):
            for o in origins:
                load_w(o, g).start()
            return 0

        lax.fori_loop(0, n_chunks, body, 0)

    start_w([t, sibling])
    start_w(behind + behind_sib)

    lax.fori_loop(0, n_chunks, wait_q, 0)
    acc[...] = jnp.zeros_like(acc)
    def make_within(g):
        row_ids = lax.broadcasted_iota(jnp.int32, (rows, rows), 0)
        col_ids = lax.broadcasted_iota(jnp.int32, (rows, rows), 1)
        causal = col_ids <= row_ids
        for h in range(PACK):
            cols = pl.ds(h * DH, DH)
            scores = lax.dot_general(
                q_buf[g, :, cols], k_buf[g, :, cols], (((1,), (1,)), ((), ())),
                preferred_element_type=F32,
            )
            scores = jnp.where(causal, scores, 0.0).astype(BF16)
            within[g, :, cols] = jnp.dot(scores, v_buf[g, :, cols], preferred_element_type=F32)

    n_cols = acc.shape[1]
    tile = min(512, n_cols)

    def project(pieces):
        for o, g in pieces:
            load_w(o, g).wait()
        for at in range(0, n_cols, tile):
            cols = pl.ds(at, tile)
            total = acc[:, cols]
            for o, g in pieces:
                total += jnp.dot(
                    normed[o, g], w_buf[o * n_chunks + g, :, cols], preferred_element_type=F32
                )
            acc[:, cols] = total

    make_within(0)

    def step(g, _):
        copy_x(g).wait_recv()

        @pl.when(has_before)
        def _():
            copy_z(g).wait_recv()

        later = inner > 0
        for h in range(PACK):
            other = x_in[g, h].astype(F32)
            before = jnp.where(has_before, z_in[g, h].astype(F32), 0.0)
            z_out[g, h] = (before + (state[g, h] + other)).astype(z_out.dtype)
            state[g, h] = before + jnp.where(later, other, 0.0)

        @pl.when(has_after)
        def _():
            copy_z(g).start()

        for h in range(PACK):
            cols = pl.ds(h * DH, DH)
            prefix = state[g, h].astype(BF16)
            attended = within[g, :, cols] + jnp.dot(
                q_buf[g, :, cols], prefix, preferred_element_type=F32
            )
            inverse = lax.rsqrt(jnp.mean(attended * attended, axis=-1, keepdims=True) + EPSILON)
            normed[t, g, :, cols] = (attended * inverse * gain_ref[...]).astype(BF16)
        for d in range(n_y - 1):
            copy_y(d, g).start()
        copy_sib(g).start()

        make_within(jnp.minimum(g + 1, n_chunks - 1))

        @pl.when(g > 0)
        def _():
            arrived(sibling, g - 1).wait_recv()
            project([(t, g - 1), (sibling, g - 1)])

        return 0

    lax.fori_loop(0, n_chunks, step, 0)
    last = n_chunks - 1
    arrived(sibling, last).wait_recv()
    project([(t, last), (sibling, last)])

    def collect(g, _):
        for d in range(n_y - 1):
            arrived(behind[d], g).wait_recv()
            copy_fwd(d, g).start()

        @pl.when(g > 0)
        def _():
            for d in range(n_y - 1):
                arrived(behind_sib[d], g - 1).wait_recv()
                project([(behind[d], g - 1), (behind_sib[d], g - 1)])

        return 0

    lax.fori_loop(0, n_chunks, collect, 0)
    for d in range(n_y - 1):
        project([(behind[d], last)])
        arrived(behind_sib[d], last).wait_recv()
        project([(behind_sib[d], last)])
    o_ref[...] = acc[...].astype(o_ref.dtype)

    def drain(g, _):
        copy_x(g).wait_send()

        @pl.when(has_after)
        def _():
            copy_z(g).wait_send()

        copy_sib(g).wait_send()
        for d in range(n_y - 1):
            copy_y(d, g).wait_send()
            copy_fwd(d, g).wait_send()
        return 0

    lax.fori_loop(0, n_chunks, drain, 0)


def on_device(n_seq, n_tp, queries, keys, values, norm_gain, out_weight):
    rows, own = queries.shape
    depth, n_cols = out_weight.shape
    width = PACK * DH
    n_chunks = own // width
    n_y = n_tp // 2
    link = BF16 if n_seq // INNER <= 4 else F32
    chunk = (n_chunks, rows, width)
    states = (n_chunks, PACK, DH, DH)
    vmem = pl.BlockSpec(memory_space=pltpu.VMEM)
    hbm = pl.BlockSpec(memory_space=pltpu.HBM)
    dma = pltpu.SemaphoreType.DMA
    flops = 2 * rows * depth * n_cols + 2 * rows * own * (2 * rows + 2 * DH)
    return pl.pallas_call(
        functools.partial(kernel, n_seq, n_tp),
        out_shape=jax.ShapeDtypeStruct((rows, n_cols), BF16),
        in_specs=[hbm, hbm, hbm, vmem, hbm],
        out_specs=vmem,
        scratch_shapes=[
            pltpu.VMEM(chunk, BF16),
            pltpu.VMEM(chunk, BF16),
            pltpu.VMEM(chunk, BF16),
            pltpu.VMEM((depth // width, width, n_cols), BF16),
            pltpu.VMEM(states, F32),
            pltpu.VMEM(states, link),
            pltpu.VMEM(states, link),
            pltpu.VMEM(states, link),
            pltpu.VMEM(states, link),
            pltpu.VMEM(chunk, F32),
            pltpu.VMEM((n_tp,) + chunk, BF16),
            pltpu.VMEM((rows, n_cols), F32),
            dma((3, n_chunks)),
            dma((depth // width,)),
            dma((n_chunks,)),
            dma((n_chunks,)),
            dma((n_chunks,)),
            dma((n_chunks,)),
            dma((n_chunks,)),
            dma((n_y - 1, n_chunks)),
            dma((n_y - 1, n_chunks)),
            dma((n_tp, n_chunks)),
        ],
        compiler_params=pltpu.CompilerParams(
            collective_id=0, has_side_effects=True, vmem_limit_bytes=60 * 1024 * 1024
        ),
        cost_estimate=pl.CostEstimate(
            flops=flops, bytes_accessed=2 * (depth * n_cols + 4 * rows * own), transcendentals=0
        ),
    )(queries, keys, values, norm_gain.reshape(1, DH), out_weight)


def solution(mesh):
    n_seq, n_tp = mesh.shape["seq"], mesh.shape["tp"]
    return jax.shard_map(
        functools.partial(on_device, n_seq, n_tp),
        mesh=mesh,
        in_specs=(P("seq", "tp"), P("seq", "tp"), P("seq", "tp"), P(), P(None, "tp")),
        out_specs=P("seq", "tp"),
        check_vma=False,
    )
```

time: 179 us -> 45.3 us (0.25)
  waiting for transfers between devices: 128 us -> 0 us
  Pallas kernels: 0 us -> 42.8 us
  matrix products: 25.4 us -> 0 us
  between operations: 13.5 us -> 0.01 us
  starting transfers between devices: 5.7 us -> 0 us
  other arithmetic: 2.77 us -> 0 us
    ppermute x3 -> x0, waiting for transfers between devices: 92.7 us -> none  [from_behind(): return lax.ppermute(x, axis, pairs)]
    pallas_call x0 -> x1, Pallas kernels: none -> 42.8 us  [on_device(): pl.pallas_call(functools.partial(kernel, n_seq, n_tp), out_shape=jax.Shap...]
    all_gather x1 -> x0, waiting for transfers between devices: 34.9 us -> none  [on_device(): collected_states = lax.all_gather(normed, 'tp', axis=1, tiled=True)]
    dot_general x4 -> x0, matrix products: 25.4 us -> none  [the longest x1 17 us: on_device(): jnp.dot(collected_states, out_weight, preferred_element_type=jnp.float32)]
    ppermute x3 -> x0, starting transfers between devices: 5.69 us -> none  [from_behind(): return lax.ppermute(x, axis, pairs)]
    reshape x2 -> x0, local copies, waits for them, and re-layouts: 2.93 us -> none  [the longest x1 1.62 us: on_device(): value_head_rows = values.reshape(tok_rows, head_count, DH)]
    unnamed x6 -> x1, local copies, waits for them, and re-layouts: 0.01 us -> 2.3 us
  transfers between devices with their start and end apart: 4 -> 0, of which waited for: 4 -> 0; matrix products, arithmetic and copies ran while one was open for 2% -> 0% of each run, Pallas kernels for 0% -> 0%
where the time goes in v1:
time: 45.3 us; the launch traced here: 45.1 us
  Pallas kernels  42.8 us (94%)
  local copies, waits for them, and re-layouts  2.3 us (5%)
    pallas_call x1, Pallas kernels, on_device(): pl.pallas_call(functools.partial(kernel, n_seq, n_tp), out_shape=jax.Shap...  42.8 us
    unnamed x1, local copies, waits for them, and re-layouts  2.3 us

profile of v1, /device:TPU:25, one launch (start us, length us, event | category | flops | bytes accessed | tf_op | source)
XLA Modules:
  0.0 45.1 jit_solution(2291722151125080913)
XLA Ops:
  0.0 42.8 %shard_map.55 = bf16[256,2048]{1,0:T(8,128)(2,1)} custom-call(bf16[256,2048]{1,0:T(8,128)(2,1)} %q_hbm.1, bf16[256,2048]{1,0:T(8,128)(2,1)} %k_hbm.1, bf16[256,2048]{1,0:T(8,128)(2,1)} %v_hbm.1, f32[1,128]{1,0:T(1,128)} %bitcast.1, bf16[8192,2048]{1,0:T(8,128)(2,1)} %w_hbm.1), custom_call_target="tpu_custom_call" | custom-call | flops 9395240960 | bytes 37748736 | tf_op jit(solution)/shard_map/pallas_call | solution.py:256
  42.8 2.3 %copy.7 = bf16[256,2048]{1,0:T(8,128)(2,1)} copy(bf16[256,2048]{1,0:T(8,128)(2,1)} %shard_map.55) | data formatting | bytes 2097152

commit v2 on v1

--- a/solution.py
+++ b/solution.py
@@ -95,6 +95,7 @@
 
     lax.fori_loop(0, n_chunks, start_q, 0)
 
+    acc[...] = jnp.zeros_like(acc)
     pl.semaphore_wait(barrier, 1 + n_y + jnp.where(has_after, 1, 0))
 
     def make_state(g, _):
@@ -109,6 +110,8 @@
             state[g, h] = own
             x_out[g, h] = own.astype(x_out.dtype)
         copy_x(g).start()
+        for o in (t, sibling):
+            load_w(o, g).start()
         return 0
 
     lax.fori_loop(0, n_chunks, make_state, 0)
@@ -117,19 +120,7 @@
         load(2, g).wait()
         return 0
 
-    def start_w(origins):
-        def body(g, _):
-            for o in origins:
-                load_w(o, g).start()
-            return 0
-
-        lax.fori_loop(0, n_chunks, body, 0)
-
-    start_w([t, sibling])
-    start_w(behind + behind_sib)
-
     lax.fori_loop(0, n_chunks, wait_q, 0)
-    acc[...] = jnp.zeros_like(acc)
     def make_within(g):
         row_ids = lax.broadcasted_iota(jnp.int32, (rows, rows), 0)
         col_ids = lax.broadcasted_iota(jnp.int32, (rows, rows), 1)
@@ -189,6 +180,8 @@
         for d in range(n_y - 1):
             copy_y(d, g).start()
         copy_sib(g).start()
+        for o in behind + behind_sib:
+            load_w(o, g).start()
 
         make_within(jnp.minimum(g + 1, n_chunks - 1))
 

time: 45.3 us -> 45.3 us (level)
  no operation moved by 1% of the time
where the time goes in v2:
time: 45.3 us; the launch traced here: 45.1 us
  Pallas kernels  42.8 us (94%)
  local copies, waits for them, and re-layouts  2.3 us (5%)
    pallas_call x1, Pallas kernels, on_device(): pl.pallas_call(functools.partial(kernel, n_seq, n_tp), out_shape=jax.Shap...  42.8 us
    unnamed x1, local copies, waits for them, and re-layouts  2.3 us

profile of v2, /device:TPU:25, one launch (start us, length us, event | category | flops | bytes accessed | tf_op | source)
XLA Modules:
  0.0 45.1 jit_solution(15231955461493576860)
XLA Ops:
  0.0 42.8 %shard_map.55 = bf16[256,2048]{1,0:T(8,128)(2,1)} custom-call(bf16[256,2048]{1,0:T(8,128)(2,1)} %q_hbm.1, bf16[256,2048]{1,0:T(8,128)(2,1)} %k_hbm.1, bf16[256,2048]{1,0:T(8,128)(2,1)} %v_hbm.1, f32[1,128]{1,0:T(1,128)} %bitcast.1, bf16[8192,2048]{1,0:T(8,128)(2,1)} %w_hbm.1), custom_call_target="tpu_custom_call" | custom-call | flops 9395240960 | bytes 37748736 | tf_op jit(solution)/shard_map/pallas_call | solution.py:249
  42.8 2.3 %copy.7 = bf16[256,2048]{1,0:T(8,128)(2,1)} copy(bf16[256,2048]{1,0:T(8,128)(2,1)} %shard_map.55) | data formatting | bytes 2097152

commit v3 on v2

--- a/solution.py
+++ b/solution.py
@@ -9,6 +9,7 @@
 
 DH = 128
 PACK = 2
+LEAD = 3
 INNER = 2
 EPSILON = 1e-06
 MESH = pl.DeviceIdType.MESH
@@ -114,7 +115,8 @@
             load_w(o, g).start()
         return 0
 
-    lax.fori_loop(0, n_chunks, make_state, 0)
+    lead = min(LEAD, n_chunks)
+    lax.fori_loop(0, lead, make_state, 0)
 
     def wait_q(g, _):
         load(2, g).wait()
@@ -185,22 +187,23 @@
 
         make_within(jnp.minimum(g + 1, n_chunks - 1))
 
-        @pl.when(g > 0)
-        def _():
-            arrived(sibling, g - 1).wait_recv()
-            project([(t, g - 1), (sibling, g - 1)])
-
-        return 0
-
-    lax.fori_loop(0, n_chunks, step, 0)
+        return 0
+
+    def step_and_state(g, _):
+        step(g, 0)
+        make_state(g + lead, 0)
+        return 0
+
+    lax.fori_loop(0, n_chunks - lead, step_and_state, 0)
+    lax.fori_loop(n_chunks - lead, n_chunks, step, 0)
     last = n_chunks - 1
-    arrived(sibling, last).wait_recv()
-    project([(t, last), (sibling, last)])
 
     def collect(g, _):
         for d in range(n_y - 1):
             arrived(behind[d], g).wait_recv()
             copy_fwd(d, g).start()
+        arrived(sibling, g).wait_recv()
+        project([(t, g), (sibling, g)])
 
         @pl.when(g > 0)
         def _():

time: 45.3 us -> 44.4 us (0.980)
  Pallas kernels: 42.8 us -> 41.7 us
    pallas_call x1, Pallas kernels: 42.8 us -> 41.7 us  [on_device(): pl.pallas_call(functools.partial(kernel, n_seq, n_tp), out_shape=jax.Shap...]
where the time goes in v3:
time: 44.4 us; the launch traced here: 44 us
  Pallas kernels  41.7 us (94%)
  local copies, waits for them, and re-layouts  2.3 us (5%)
    pallas_call x1, Pallas kernels, on_device(): pl.pallas_call(functools.partial(kernel, n_seq, n_tp), out_shape=jax.Shap...  41.7 us
    unnamed x1, local copies, waits for them, and re-layouts  2.3 us

profile of v3, /device:TPU:25, one launch (start us, length us, event | category | flops | bytes accessed | tf_op | source)
XLA Modules:
  0.0 44.0 jit_solution(4210650179547963002)
XLA Ops:
  0.0 41.7 %shard_map.55 = bf16[256,2048]{1,0:T(8,128)(2,1)} custom-call(bf16[256,2048]{1,0:T(8,128)(2,1)} %q_hbm.1, bf16[256,2048]{1,0:T(8,128)(2,1)} %k_hbm.1, bf16[256,2048]{1,0:T(8,128)(2,1)} %v_hbm.1, f32[1,128]{1,0:T(1,128)} %bitcast.1, bf16[8192,2048]{1,0:T(8,128)(2,1)} %w_hbm.1), custom_call_target="tpu_custom_call" | custom-call | flops 9395240960 | bytes 37748736 | tf_op jit(solution)/shard_map/pallas_call | solution.py:252
  41.7 2.3 %copy.7 = bf16[256,2048]{1,0:T(8,128)(2,1)} copy(bf16[256,2048]{1,0:T(8,128)(2,1)} %shard_map.55) | data formatting | bytes 2097152
